TPU v7x, 512 devices: a whole 4x8x8 slice. The times are simulated.
512 devices in a mesh: row: 32 (over z, y_hi), col: 16 (over x, y_lo, core).
Axes of the slice: x: 4, y: 8 (y_hi: 4, y_lo: 2; y = y_hi * 2 + y_lo), z: 8, core: 2. Of those that a mesh axis runs over, the one named last changes fastest.
Arguments:
- momentum: bfloat16 [4096, 14336], P('row', 'col'), may hold values from -0.098552583 to 0.098552583
Outputs:
- update: float32 [4096, 14336], P('row', 'col')
All inputs are finite; a program needn't handle non-finite values.
Results may differ from a plain program's by a relative error of at most 0.0048.
Values may be sent and summed in bfloat16 or wider, within the bound.
A program may use at most 64 MiB of HBM per device.

v0:
```python
import math

import jax
import jax.numpy as jnp
from jax import lax
from jax.sharding import PartitionSpec as P

M = 4096
N = 14336


quintic_a = 3.4445
quintic_b = -4.775
quintic_c = 2.0315


def per_device(momentum):
    col_size = lax.axis_size("col")
    whole = lax.all_gather(momentum, "row", axis=0, tiled=True)
    total_rows = whole.shape[0]
    col_width = total_rows // col_size
    place_col = lax.axis_index("col")
    partial_value = lax.dot_general(
        momentum, whole, (((1,), (1,)), ((), ())), preferred_element_type=jnp.float32
    )
    gram_row = lax.psum(partial_value, "col")
    row_half = gram_row.astype(jnp.bfloat16)
    tile_half = lax.dynamic_slice_in_dim(row_half, place_col * col_width, col_width, 1)
    square = jnp.dot(
        row_half,
        lax.all_gather(tile_half, "row", axis=0, tiled=True),
        preferred_element_type=jnp.float32,
    )
    poly_tile = (quintic_b * tile_half.astype(jnp.float32) + quintic_c * square).astype(
        jnp.bfloat16
    )
    product = jnp.dot(
        lax.all_gather(poly_tile, "col", axis=1, tiled=True),
        whole,
        preferred_element_type=jnp.float32,
    )
    return math.sqrt(max(M, N)) * (quintic_a * momentum.astype(jnp.float32) + product)


def solution(mesh):
    in_specs = (P("row", "col"),)
    out_specs = P("row", "col")
    return jax.shard_map(
        per_device, mesh=mesh, in_specs=in_specs, out_specs=out_specs, check_vma=False
    )
```

profile of v0, /device:TPU:1, one launch (start us, length us, event | category | flops | bytes accessed | tf_op | source)
XLA Modules:
  0.0 356.4 jit_solution(12447808224269611025)
XLA Ops:
  6.5 0.0 all-gather.4.cloned.1.call-start
  6.5 0.7 all-gather.4.cloned.1.call-update
  7.3 0.0 all-gather.6.cloned.1.call-start
  7.3 0.0 copy-start
  7.3 137.7 %all-gather.4.cloned.1.call-done = bf16[4096,896]{1,0:T(8,128)(2,1)} async-done(((bf16[128,896]{1,0:T(8,128)(2,1)}), bf16[4096,896]{1,0:T(8,128)(2,1)}) %all-gather.4.cloned.1.call-update) | async-done | bytes 7340048 | tf_op jit(solution)/shard_map/all_gather | solution.py:19
  145.0 5.7 %fusion.3 = f32[128,4096]{1,0:T(8,128)S(1)} fusion(bf16[128,896]{1,0:T(8,128)(2,1)} %param.1, bf16[4096,896]{1,0:T(8,128)(2,1)} %all-gather.4.cloned.1.call-done), kind=kOutput, calls=%fused_computation.6 | convolution fusion | flops 939524096 | bytes 9666560 | tf_op jit(solution)/shard_map/dot_general | solution.py:23
  150.7 71.8 %all-reduce.1 = bf16[128,4096]{1,0:T(8,128)(2,1)S(1)} all-reduce(f32[128,4096]{1,0:T(8,128)S(1)} %fusion.3), channel_id=1, replica_groups=mesh['row'=32,'col'=16] {'col'}, use_global_device_ids=true, to_apply=%region_0.0 | all-reduce | flops 524288 | bytes 3145728 | tf_op jit(solution)/shard_map/psum | solution.py:26
  222.5 0.6 constant_dynamic-slice_fusion
  223.2 0.0 all-gather.6.cloned.1.call-update
  223.2 0.0 all-gather.8.cloned.1.call-start
  223.3 80.8 %all-gather.6.cloned.1.call-done = bf16[4096,256]{1,0:T(8,128)(2,1)} async-done(((bf16[128,256]{1,0:T(8,128)(2,1)}), bf16[4096,256]{1,0:T(8,128)(2,1)}) %all-gather.6.cloned.1.call-update) | async-done | bytes 2097168 | tf_op jit(solution)/shard_map/all_gather | solution.py:31
  304.1 2.7 fusion.2
  306.7 0.0 all-gather.8.cloned.1.call-update
  306.8 37.7 %all-gather.8.cloned.1.call-done = bf16[128,4096]{1,0:T(8,128)(2,1)} async-done(((bf16[128,256]{1,0:T(8,128)(2,1)}), bf16[128,4096]{1,0:T(8,128)(2,1)}) %all-gather.8.cloned.1.call-update) | async-done | bytes 1048592 | tf_op jit(solution)/shard_map/all_gather | solution.py:38
  344.5 0.0 copy-done
  344.5 5.5 %fusion = f32[128,896]{1,0:T(8,128)} fusion(bf16[128,4096]{1,0:T(8,128)(2,1)} %all-gather.8.cloned.1.call-done, bf16[4096,896]{1,0:T(8,128)(2,1)} %all-gather.4.cloned.1.call-done, bf16[128,896]{1,0:T(8,128)(2,1)S(1)} %copy-done), kind=kOutput, calls=%fused_computation.1 | convolution fusion | flops 939982848 | bytes 9076736 | tf_op jit(solution)/shard_map/dot_general | solution.py:37
Async XLA Ops:
  6.5 138.5 %all-gather.4.cloned.1.call-start = ((), (), s32[]{:S(2)}) async-start(), calls=%async_computation | async-start | bytes 7569408 | tf_op jit(solution)/shard_map/all_gather | solution.py:19
  7.3 296.8 %all-gather.6.cloned.1.call-start = ((), (), s32[]{:S(2)}) async-start(), calls=%async_computation.1 | async-start | bytes 2162688 | tf_op jit(solution)/shard_map/all_gather | solution.py:31
  7.3 337.1 %copy-start = (bf16[128,896]{1,0:T(8,128)(2,1)S(1)}, bf16[128,896]{1,0:T(8,128)(2,1)}, u32[]{:S(2)}) copy-start(bf16[128,896]{1,0:T(8,128)(2,1)} %param.1) | copy-start | bytes 688132
  223.2 121.2 %all-gather.8.cloned.1.call-start = ((), (), s32[]{:S(2)}) async-start(), calls=%async_computation.2 | async-start | bytes 1114112 | tf_op jit(solution)/shard_map/all_gather | solution.py:38
Sparse Core Ops, SparseCore 0:
  10.5 134.4 all-gather.3
  223.3 80.6 all-gather.5
  306.9 37.5 all-gather.7
where the time goes:
time: 357 us; the launch traced here: 356 us
  waiting for transfers between devices  257 us (72%)
  blocking collectives  71.8 us (20%)
  matrix products  13.8 us (4%)
  between operations  13.1 us (4%)
    all_gather x1, waiting for transfers between devices, per_device(): whole = lax.all_gather(momentum, 'row', axis=0, tiled=True)  138 us
    all_gather x1, waiting for transfers between devices, per_device(): lax.all_gather(tile_half, 'row', axis=0, tiled=True)  80.8 us
    psum x1, blocking collectives, per_device(): gram_row = lax.psum(partial_value, 'col')  71.8 us
    all_gather x1, waiting for transfers between devices, per_device(): lax.all_gather(poly_tile, 'col', axis=1, tiled=True)  37.7 us
  transfers between devices with their start and end apart: 3, of which 3 were waited for; matrix products, arithmetic and copies ran while one was open for 0% of the time, Pallas kernels for 0%

commit v1 on v0

v1 whole, which is shorter than its diff:
```python
import math

import jax
import jax.numpy as jnp
from jax import lax
from jax.experimental import pallas as pl
from jax.experimental.pallas import tpu as pltpu
from jax.sharding import PartitionSpec as P

M = 4096
N = 14336
quintic_a = 3.4445
quintic_b = -4.775
quintic_c = 2.0315

NZ, NYH, NX, NYL = 8, 4, 4, 2
NY = NYH * NYL
R = 128
C = 896
H = R // 2
W = 256
CZ = 384
CY = C - CZ
SEMS = 200

F32 = jnp.float32
BF16 = jnp.bfloat16


def kernel(
    x_ref, out_ref,
    xi, xj, acc, sib_out, sib_in, rs_out, rs_in, ga, gb, pb, pt,
    zs_out, zs_in, ys_out, ys_in, zown, yown,
    send_sems, recv_sems,
):
    row = lax.axis_index("row")
    col = lax.axis_index("col")
    z, yh = row // NYH, row % NYH
    q, h = col // 2, col % 2
    x, yl = q // NYL, q % NYL
    y = yh * NYL + yl

    def device(z=z, y=y, x=x, h=h):
        return (z * NYH + y // NYL, (x * NYL + y % NYL) * 2 + h)

    def zmod(d):
        return (z + d + NZ) % NZ

    def ymod(d):
        return (y + d + NY) % NY

    def yhmod(d):
        return (yh + d + NYH) % NYH

    z_dev = {1: device(z=zmod(1)), -1: device(z=zmod(-1))}
    y_dev = {1: device(y=ymod(1)), -1: device(y=ymod(-1))}
    yh_dev = {1: device(y=ymod(2)), -1: device(y=ymod(-2))}
    sibling = device(h=1 - h)

    def q_dev(k):
        dx, dy = k // 2, k % 2
        return device(x=(x + dx) % NX, y=yh * NYL + (yl + dy) % NYL)

    def q_of(k):
        dx, dy = k // 2, k % 2
        return ((x + dx) % NX) * NYL + (yl + dy) % NYL

    pending = []
    count = [0]

    def send(src, dst, to):
        n = count[0]
        count[0] += 1
        copy = pltpu.make_async_remote_copy(
            src_ref=src, dst_ref=dst, send_sem=send_sems.at[n], recv_sem=recv_sems.at[n],
            device_id=to, device_id_type=pl.DeviceIdType.MESH,
        )
        copy.start()
        pending.append(copy)
        return copy

    barrier = pltpu.get_barrier_semaphore()
    partners = [z_dev[1], z_dev[-1], yh_dev[1], yh_dev[-1], y_dev[1], y_dev[-1], sibling]
    partners += [q_dev(k) for k in range(1, 8)]
    for partner in partners:
        pl.semaphore_signal(barrier, inc=1, device_id=partner, device_id_type=pl.DeviceIdType.MESH)
    pl.semaphore_wait(barrier, len(partners))

    top, low = pl.ds(0, H), pl.ds(H, H)
    halves = (top, low)
    zc, yc = {}, {}
    for c in range(2):
        for d in (1, -1):
            zc[d, 1, c] = send(x_ref.at[halves[c]], xi.at[z, halves[c]], z_dev[d])
            yc[d, 1, c] = send(x_ref.at[halves[c]], xj.at[yh, halves[c]], yh_dev[d])
    xi[z] = x_ref[...]
    xj[yh] = x_ref[...]

    def z_step(s, c):
        for d in (1, -1):
            if (d, s, c) not in zc:
                continue
            zc[d, s, c].wait_recv()
            if s < 3 or (s == 3 and c == (0 if d == 1 else 1)):
                held = xi.at[zmod(-d * s), halves[c]]
                zc[d, s + 1, c] = send(held, held, z_dev[d])

    def y_step(s, c):
        for d in (1, -1):
            if (d, s, c) not in yc:
                continue
            yc[d, s, c].wait_recv()
            if s == 1 and c == (0 if d == 1 else 1):
                held = xj.at[yhmod(-d), halves[c]]
                yc[d, 2, c] = send(held, held, yh_dev[d])

    z_step(1, 0)
    z_step(1, 1)
    y_step(1, 0)
    z_step(2, 0)
    z_step(2, 1)
    y_step(1, 1)
    z_step(3, 0)
    z_step(3, 1)
    y_step(2, 0)
    y_step(2, 1)

    def gram(zz, own):
        left = xi[zz]
        for half in range(2):
            right = xj[2 * half : 2 * half + 2].reshape(W, C)
            value = lax.dot_general(left, right, (((1,), (1,)), ((), ())), preferred_element_type=F32)

            @pl.when(h == half)
            def _():
                acc[zz] = value

            @pl.when(h != half)
            def _():
                sib_out[zz] = value

    z_step(4, 0)
    z_step(4, 1)
    sib = {}
    order = [1, 2, 3, 4, 5, 6, 7, 0]
    for k in order:
        zz = q_of(k)
        gram(zz, None)
        sib[k] = send(sib_out.at[zz], sib_in.at[zz], sibling)
    rs = {}
    for k in order:
        zz = q_of(k)
        sib[k].wait_recv()
        total = acc[zz] + sib_in[zz]
        if k:
            rs_out[k] = total.astype(BF16)
            rs[k] = send(rs_out.at[k], rs_in.at[k], q_dev(k))
        else:
            acc[q] = total
    total = acc[q]
    for k in range(1, 8):
        rs[k].wait_recv()
        total = total + rs_in[k].astype(F32)
    gram_own = total.astype(BF16)
    gb[x, y] = gram_own
    ga[z, h] = gram_own

    bc, ac, bx, ax, gz, gs = {}, {}, {}, {}, {}, {}
    quarters = (pl.ds(H, H // 2), pl.ds(H + H // 2, H // 2))
    for d in (1, -1):
        bc[d, 1] = send(gb.at[x, y, low], gb.at[x, y, low], y_dev[d])
    for dx in (1, 3, 2):
        ax[dx] = send(gb.at[x, y, top], gb.at[x, y, top], device(x=(x + dx) % NX))
    for d in (1, -1):
        ac[d, 1, 0] = send(gb.at[x, y, top], gb.at[x, y, top], y_dev[d])
    for d in (1, -1):
        gz[d, 1] = send(ga.at[z, h], ga.at[z, h], z_dev[d])
    for dx in (1, 3, 2):
        bx[0, dx] = send(gb.at[x, y, low], gb.at[x, y, low], device(x=(x + dx) % NX))
    gs[0] = send(ga.at[z, h], ga.at[z, h], sibling)
    zrows = (pl.ds(0, H), pl.ds(H, H))

    def b_step(s):
        for d in (1, -1):
            bc[d, s].wait_recv()
            if s < 3:
                held = gb.at[x, ymod(-d * s), low]
                bc[d, s + 1] = send(held, held, y_dev[d])
            elif s == 3:
                held = gb.at[x, ymod(-d * s), quarters[0 if d == 1 else 1]]
                bc[d, 4] = send(held, held, y_dev[d])
        for d in (1, -1) if s < 4 else (1,):
            held = gb.at[x, ymod(-d * s), low]
            for dx in (1, 3, 2):
                bx[d * s, dx] = send(held, held, device(x=(x + dx) % NX))

    def gz_step(s):
        for d in (1, -1):
            gz[d, s].wait_recv()
            if s < 3:
                held = ga.at[zmod(-d * s), h]
                gz[d, s + 1] = send(held, held, z_dev[d])
            elif s == 3:
                held = ga.at[zmod(-d * s), h, zrows[0 if d == 1 else 1]]
                gz[d, 4] = send(held, held, z_dev[d])
        for d in (1, -1) if s < 4 else (1,):
            held = ga.at[zmod(-d * s), h]
            gs[d * s] = send(held, held, sibling)

    def a_step(s, rx):
        for d in (1, -1):
            if s == 0:
                if d == 1:
                    ax[rx].wait_recv()
            elif (d, s, rx) in ac:
                ac[d, s, rx].wait_recv()
            else:
                continue
            if s < 3 or (s == 3 and (rx in (0, 1)) == (d == 1)):
                held = gb.at[(x - rx + NX) % NX, ymod(-d * s), top]
                ac[d, s + 1, rx] = send(held, held, y_dev[d])

    b_step(1)
    for rx in (1, 3, 2):
        a_step(0, rx)
    gz_step(1)
    a_step(1, 0)
    b_step(2)
    for rx in (1, 3, 2):
        a_step(1, rx)
    gz_step(2)
    a_step(2, 0)
    b_step(3)
    for rx in (1, 3, 2):
        a_step(2, rx)
    gz_step(3)
    b_step(4)
    gz_step(4)
    for rx in (0, 1, 3, 2):
        a_step(3, rx)
    for rx in (0, 1, 3, 2):
        a_step(4, rx)
    for copy in bx.values():
        copy.wait_recv()
    for copy in gs.values():
        copy.wait_recv()

    def square(qq, total):
        xx, yy = qq // NYL, qq % NYL
        for half in range(2):
            right = jnp.concatenate(
                [gb[xx, 4 * half + yy], gb[xx, 4 * half + 2 + yy]], axis=0
            )
            total = total + jnp.dot(ga[qq, half], right, preferred_element_type=F32)
        return total

    total = jnp.zeros((R, W), F32)
    for qq in range(8):
        total = square(qq, total)
    poly = (quintic_b * gb[x, y].astype(F32) + quintic_c * total).astype(BF16)
    pb[q, h] = poly

    pc, ps = {}, {}
    for k in (2, 6, 1, 4, 3, 7, 5):
        pc[k] = send(pb.at[q, h], pb.at[q, h], q_dev(k))
    ps[0] = send(pb.at[q, h], pb.at[q, h], sibling)
    for k in (2, 6, 1, 4, 3, 7, 5):
        dx, dy = k // 2, k % 2
        held = pb.at[((x - dx + NX) % NX) * NYL + (yl + dy) % NYL, h]
        pc[k].wait_recv()
        ps[k] = send(held, held, sibling)
    for copy in ps.values():
        copy.wait_recv()

    for qq in range(8):
        for half in range(2):
            turned = pb[qq, half].astype(F32).T.astype(BF16)
            for part in range(2):
                pt[2 * half + part, :, qq * R : (qq + 1) * R] = turned[part * R : (part + 1) * R]

    def z_part(zz, rows):
        value = 0.0
        for half in range(2):
            right = xj[2 * half : 2 * half + 2, :, 0:CZ].reshape(W, CZ)
            value = value + jnp.dot(pb[zz, half, rows], right, preferred_element_type=F32)
        return value

    def y_part(yy, rows):
        right = xi[:, :, CZ:C].reshape(NZ * R, CY)
        return jnp.dot(pt[yy, rows], right, preferred_element_type=F32)

    zr, yr = {}, {}

    def first(d):
        return 0 if d == 1 else 1

    def z_send(d, s, c, value):
        n = 0 if d == 1 else 1
        zs_out[n, s, halves[c]] = value.astype(BF16)
        zr[d, s, c] = send(zs_out.at[n, s, halves[c]], zs_in.at[n, s, halves[c]], z_dev[d])

    def y_send(d, s, c, value):
        n = 0 if d == 1 else 1
        ys_out[n, s, halves[c]] = value.astype(BF16)
        yr[d, s, c] = send(ys_out.at[n, s, halves[c]], ys_in.at[n, s, halves[c]], yh_dev[d])

    def z_got(d, s, c):
        zr[d, s, c].wait_recv()
        return zs_in[0 if d == 1 else 1, s, halves[c]].astype(F32)

    def y_got(d, s, c):
        yr[d, s, c].wait_recv()
        return ys_in[0 if d == 1 else 1, s, halves[c]].astype(F32)

    for d in (1, -1):
        z_send(d, 0, first(d), z_part(zmod(4 * d), halves[first(d)]))
    for d in (1, -1):
        y_send(d, 0, first(d), y_part(yhmod(2 * d), halves[first(d)]))
    for d in (1, -1):
        z_send(d, 1, 1 - first(d), z_part(zmod(3 * d), halves[1 - first(d)]))
    for d in (1, -1):
        y_send(d, 1, 1 - first(d), y_part(yhmod(d), halves[1 - first(d)]))
    for d in (1, -1):
        c = first(d)
        z_send(d, 1, c, z_part(zmod(3 * d), halves[c]) + z_got(d, 0, c))
    for d in (1, -1):
        c = 1 - first(d)
        z_send(d, 2, c, z_part(zmod(2 * d), halves[c]) + z_got(d, 1, c))
    for d in (1, -1):
        c = first(d)
        y_send(d, 1, c, y_part(yhmod(d), halves[c]) + y_got(d, 0, c))
    for d in (1, -1):
        c = first(d)
        z_send(d, 2, c, z_part(zmod(2 * d), halves[c]) + z_got(d, 1, c))
    for d in (1, -1):
        c = 1 - first(d)
        z_send(d, 3, c, z_part(zmod(d), halves[c]) + z_got(d, 2, c))
    for d in (1, -1):
        c = first(d)
        z_send(d, 3, c, z_part(zmod(d), halves[c]) + z_got(d, 2, c))

    zown[...] = z_part(z, pl.ds(0, R))
    yown[...] = y_part(yh, pl.ds(0, R))
    scale = math.sqrt(max(M, N))
    for c in (0, 1):
        rows = halves[c]
        value = yown[rows] + y_got(1, 1, c) + y_got(-1, 1, c)
        out_ref[rows, CZ:C] = scale * (quintic_a * x_ref[rows, CZ:C].astype(F32) + value)
    for c in (0, 1):
        rows = halves[c]
        value = zown[rows] + z_got(1, 3, c) + z_got(-1, 3, c)
        out_ref[rows, 0:CZ] = scale * (quintic_a * x_ref[rows, 0:CZ].astype(F32) + value)

    for copy in pending:
        copy.wait_send()


def per_device(momentum):
    return pl.pallas_call(
        kernel,
        out_shape=jax.ShapeDtypeStruct((R, C), F32),
        in_specs=[pl.BlockSpec(memory_space=pltpu.VMEM)],
        out_specs=pl.BlockSpec(memory_space=pltpu.VMEM),
        scratch_shapes=[
            pltpu.VMEM((NZ, R, C), BF16),
            pltpu.VMEM((NYH, R, C), BF16),
            pltpu.VMEM((NZ, R, W), F32),
            pltpu.VMEM((NZ, R, W), F32),
            pltpu.VMEM((NZ, R, W), F32),
            pltpu.VMEM((NZ, R, W), BF16),
            pltpu.VMEM((NZ, R, W), BF16),
            pltpu.VMEM((NZ, 2, R, W), BF16),
            pltpu.VMEM((NX, NY, R, W), BF16),
            pltpu.VMEM((NZ, 2, R, W), BF16),
            pltpu.VMEM((NYH, R, NZ * R), BF16),
            pltpu.VMEM((2, 4, R, CZ), BF16),
            pltpu.VMEM((2, 4, R, CZ), BF16),
            pltpu.VMEM((2, 2, R, CY), BF16),
            pltpu.VMEM((2, 2, R, CY), BF16),
            pltpu.VMEM((R, CZ), F32),
            pltpu.VMEM((R, CY), F32),
            pltpu.SemaphoreType.DMA((SEMS,)),
            pltpu.SemaphoreType.DMA((SEMS,)),
        ],
        compiler_params=pltpu.CompilerParams(
            collective_id=0, has_side_effects=True, vmem_limit_bytes=48 * 1024 * 1024
        ),
        cost_estimate=pl.CostEstimate(flops=2200000000, bytes_accessed=1000000, transcendentals=0),
        name="newton_schulz",
    )(momentum)


def solution(mesh):
    return jax.shard_map(
        per_device, mesh=mesh, in_specs=(P("row", "col"),), out_specs=P("row", "col"), check_vma=False
    )
```

time: 357 us -> 99.6 us (0.28)
  waiting for transfers between devices: 257 us -> 0 us
  Pallas kernels: 0 us -> 97.8 us
  blocking collectives: 71.8 us -> 0 us
  matrix products: 13.8 us -> 0 us
  between operations: 13.1 us -> 0.01 us
    all_gather x3 -> x0, waiting for transfers between devices: 256 us -> none  [the longest x1 138 us: per_device(): whole = lax.all_gather(momentum, 'row', axis=0, tiled=True)]
    pallas_call x0 -> x1, Pallas kernels: none -> 97.8 us  [per_device(): pl.pallas_call(kernel, out_shape=jax.ShapeDtypeStruct((R, C), F32), in_sp...]
    psum x1 -> x0, blocking collectives: 71.8 us -> none  [per_device(): gram_row = lax.psum(partial_value, 'col')]
    dot_general x3 -> x0, matrix products: 13.8 us -> none  [the longest x1 5.67 us: per_device(): lax.dot_general(momentum, whole, (((1,), (1,)), ((), ())), preferred_elem...]
  transfers between devices with their start and end apart: 3 -> 0, of which waited for: 3 -> 0; matrix products, arithmetic and copies ran while one was open for 0% -> 0% of each run, Pallas kernels for 0% -> 0%
where the time goes in v1:
time: 99.6 us; the launch traced here: 99.5 us
  Pallas kernels  97.8 us (98%)
  local copies, waits for them, and re-layouts  1.71 us (2%)
    pallas_call x1, Pallas kernels, per_device(): pl.pallas_call(kernel, out_shape=jax.ShapeDtypeStruct((R, C), F32), in_sp...  97.8 us

profile of v1, /device:TPU:1, one launch (start us, length us, event | category | flops | bytes accessed | tf_op | source)
XLA Modules:
  0.0 99.5 jit_solution(8149067469246364032)
XLA Ops:
  0.0 0.0 copy-start
  0.0 0.9 copy-done
  0.9 97.8 %newton_schulz.1 = f32[128,896]{1,0:T(8,128)S(1)} custom-call(bf16[128,896]{1,0:T(8,128)(2,1)S(1)} %copy-done), custom_call_target="tpu_custom_call" | custom-call | flops 2200000000 | bytes 1000000 | tf_op jit(solution)/shard_map/newton_schulz/pallas_call | solution.py:359
  98.7 0.8 copy.3
Async XLA Ops:
  0.0 0.9 copy-start

commit v2 on v1

v2 whole, which is shorter than its diff:
```python
import math

import jax
import jax.numpy as jnp
from jax import lax
from jax.experimental import pallas as pl
from jax.experimental.pallas import tpu as pltpu
from jax.sharding import PartitionSpec as P

M = 4096
N = 14336
quintic_a = 3.4445
quintic_b = -4.775
quintic_c = 2.0315

NZ, NYH, NX, NYL = 8, 4, 4, 2
NY = NYH * NYL
R = 128
C = 896
H = R // 2
W = 256
CZ = 384
CY = C - CZ
SEMS = 230
CHZ = 4
CHY = 2
HA = 48

F32 = jnp.float32
BF16 = jnp.bfloat16


def kernel(
    x_ref, out_ref,
    xi, xj, acc, sib_out, sib_in, rs_own, rs_out, rs_in, ga, gb, pb, pt,
    zs_out, zs_in, ys_out, ys_in, zp, yp,
    send_sems, recv_sems, rs_send, rs_recv, sib_send, sib_recv, local_sems,
):
    row = lax.axis_index("row")
    col = lax.axis_index("col")
    z, yh = row // NYH, row % NYH
    q, h = col // 2, col % 2
    x, yl = q // NYL, q % NYL
    y = yh * NYL + yl

    def device(z=z, y=y, x=x, h=h):
        return (z * NYH + y // NYL, (x * NYL + y % NYL) * 2 + h)

    def zmod(d):
        return (z + d + NZ) % NZ

    def ymod(d):
        return (y + d + NY) % NY

    def yhmod(d):
        return (yh + d + NYH) % NYH

    z_dev = {1: device(z=zmod(1)), -1: device(z=zmod(-1))}
    y_dev = {1: device(y=ymod(1)), -1: device(y=ymod(-1))}
    yh_dev = {1: device(y=ymod(2)), -1: device(y=ymod(-2))}
    sibling = device(h=1 - h)

    def q_dev(k):
        dx, dy = k // 2, k % 2
        return device(x=(x + dx) % NX, y=yh * NYL + (yl + dy) % NYL)

    def q_of(k):
        dx, dy = k // 2, k % 2
        return ((x + dx) % NX) * NYL + (yl + dy) % NYL

    pending = []
    count = [0]

    def send(src, dst, to):
        n = count[0]
        count[0] += 1
        copy = pltpu.make_async_remote_copy(
            src_ref=src, dst_ref=dst, send_sem=send_sems.at[n], recv_sem=recv_sems.at[n],
            device_id=to, device_id_type=pl.DeviceIdType.MESH,
        )
        copy.start()
        pending.append(copy)
        return copy

    barrier = pltpu.get_barrier_semaphore()
    partners = [z_dev[1], z_dev[-1], yh_dev[1], yh_dev[-1], y_dev[1], y_dev[-1], sibling]
    partners += [q_dev(k) for k in range(1, 8)] + [device(z=zmod(2)), device(z=zmod(-2))]
    for partner in partners:
        pl.semaphore_signal(barrier, inc=1, device_id=partner, device_id_type=pl.DeviceIdType.MESH)
    pl.semaphore_wait(barrier, len(partners))

    top, low = pl.ds(0, H), pl.ds(H, H)
    halves = (top, low)
    cz = [pl.ds(c * R // CHZ, R // CHZ) for c in range(CHZ)]
    cy = [pl.ds(c * R // CHY, R // CHY) for c in range(CHY)]
    zc, yc = {}, {}
    for c in range(max(CHZ, CHY)):
        for d in (1, -1):
            if c < CHZ:
                zc[d, 1, c] = send(x_ref.at[cz[c]], xi.at[z, cz[c]], z_dev[d])
        for d in (1, -1):
            if c < CHY:
                yc[d, 1, c] = send(x_ref.at[cy[c]], xj.at[yh, cy[c]], yh_dev[d])
    local = [
        pltpu.make_async_copy(x_ref, xi.at[z], local_sems.at[0]),
        pltpu.make_async_copy(x_ref, xj.at[yh], local_sems.at[1]),
    ]
    for copy in local:
        copy.start()

    def z_step(s, c):
        for d in (1, -1):
            if (d, s, c) not in zc:
                continue
            zc[d, s, c].wait_recv()
            if s < 3 or (s == 3 and (2 * c < CHZ) == (d == 1)):
                held = xi.at[zmod(-d * s), cz[c]]
                zc[d, s + 1, c] = send(held, held, z_dev[d])

    def y_step(s, c):
        for d in (1, -1):
            if (d, s, c) not in yc:
                continue
            yc[d, s, c].wait_recv()
            if s == 1 and (2 * c < CHY) == (d == 1):
                held = xj.at[yhmod(-d), cy[c]]
                yc[d, 2, c] = send(held, held, yh_dev[d])

    def sib_copy(zz, yb):
        return pltpu.make_async_remote_copy(
            src_ref=sib_out.at[zz, yb], dst_ref=sib_in.at[zz, yb],
            send_sem=sib_send.at[zz, yb], recv_sem=sib_recv.at[zz, yb],
            device_id=sibling, device_id_type=pl.DeviceIdType.MESH,
        )

    def rs_copy(to, slot, bit):
        return pltpu.make_async_remote_copy(
            src_ref=rs_out.at[to, bit], dst_ref=rs_in.at[slot, bit],
            send_sem=rs_send.at[to, bit], recv_sem=rs_recv.at[slot, bit],
            device_id=device(x=to // NYL, y=yh * NYL + to % NYL),
            device_id_type=pl.DeviceIdType.MESH,
        )

    def gram(offsets, blocks):
        left = jnp.concatenate([xi[zmod(a)] for a in offsets], axis=0)
        right = jnp.concatenate([xj[yhmod(b)] for b in blocks], axis=0)
        value = lax.dot_general(left, right, (((1,), (1,)), ((), ())), preferred_element_type=F32)
        for n, a in enumerate(offsets):
            for m, b in enumerate(blocks):
                part = value[n * R : (n + 1) * R, m * R : (m + 1) * R]
                zz, yb = zmod(a), yhmod(b)

                @pl.when(yb // 2 == h)
                def _():
                    acc[zz, yb % 2] = part

                @pl.when(yb // 2 != h)
                def _():
                    sib_out[zz, yb] = part
                    sib_copy(zz, yb).start()

    def rs_step(offsets, blocks):
        for a in offsets:
            for b in blocks:
                zz, yb = zmod(a), yhmod(b)

                @pl.when(yb // 2 == h)
                def _():
                    sib_copy(zz, yb).wait_recv()
                    total = acc[zz, yb % 2] + sib_in[zz, yb]

                    @pl.when(zz == q)
                    def _():
                        rs_own[yb % 2] = total

                    @pl.when(zz != q)
                    def _():
                        rs_out[zz, yb % 2] = total.astype(BF16)
                        rs_copy(zz, q, yb % 2).start()

    near = [0, 1, -1]
    for c in range(CHZ):
        z_step(1, c)
    z_step(2, 0)
    z_step(2, 1)
    y_step(1, 0)
    z_step(2, 2)
    z_step(2, 3)
    y_step(1, 1)
    for copy in local:
        copy.wait()
    gram([0, 1, -1], near)
    z_step(3, 0)
    z_step(3, 1)
    gram([2, -2], near)
    z_step(3, 2)
    z_step(3, 3)
    rs_step([1, -1, 0], near)
    gram([3, -3], near)
    rs_step([2, -2], near)
    y_step(2, 0)
    y_step(2, 1)
    gram([3, -3, 0, 1, -1, 2, -2], [2])
    rs_step([3, -3], near)
    rs_step([3, -3, 0, 1, -1, 2, -2], [2])
    for c in range(CHZ):
        z_step(4, c)
    gram([4], [0, 1, -1, 2])
    rs_step([4], [0, 1, -1, 2])
    for k in (2, 6, 1, 4, 3, 7, 5):
        for bit in range(2):
            rs_copy(q_of(k), q_of(k), bit).wait_recv()
    for bit in range(2):
        total = rs_own[bit]
        for k in range(1, 8):
            total = total + rs_in[q_of(k), bit].astype(F32)
        gram_own = total.astype(BF16)
        gb[x, y, :, bit * R : (bit + 1) * R] = gram_own
        ga[z, h, :, bit * R : (bit + 1) * R] = gram_own

    def xmod(d):
        return (x + d + NX) % NX

    bc, ac, bx, ax, gz, gs = {}, {}, {}, {}, {}, {}
    head, tail = pl.ds(0, HA), pl.ds(HA, R - HA)
    parts = {1: pl.ds(HA, 48), -1: pl.ds(HA + 48, R - HA - 48)}
    zhalf = {1: pl.ds(0, H), -1: pl.ds(H, H)}
    y_far = {1: device(y=ymod(2)), -1: device(y=ymod(-2))}
    z_far = {1: device(z=zmod(2)), -1: device(z=zmod(-2))}
    x_dev = {d: device(x=xmod(d)) for d in (1, -1, 2)}

    def b_cross(s, direct):
        held = gb.at[x, ymod(-s), tail]
        for d in (1, -1):
            bx[s, d] = send(held, held, x_dev[d])
        if direct:
            bx[s, 2] = send(held, held, x_dev[2])

    def b_relay(s):
        for d in (1, -1):
            bx[s, d].wait_recv()
            held = gb.at[xmod(-d), ymod(-s), parts[d]]
            bx[s, 2 * d] = send(held, held, x_dev[d])

    mine = gb.at[x, y, tail]
    for d in (1, -1):
        bc[d, 2] = send(mine, mine, y_far[d])
    mine = gb.at[x, y, head]
    for d in (1, -1, 2):
        ax[d] = send(mine, mine, x_dev[d])
    mine = gb.at[x, y, tail]
    for d in (1, -1):
        bc[d, 1] = send(mine, mine, y_dev[d])
    mine = ga.at[z, h]
    for d in (1, -1):
        gz[d, 2] = send(mine, mine, z_far[d])
    for d in (1, -1):
        gz[d, 1] = send(mine, mine, z_dev[d])
    b_cross(0, False)
    mine = gb.at[x, y, head]
    for d in (1, -1):
        ac[d, 1, 0] = send(mine, mine, y_dev[d])
    mine = ga.at[z, h]
    gs[0] = send(mine, mine, sibling)

    def b_step(s):
        for d in (1, -1):
            bc[d, s].wait_recv()
            if s == 2:
                held = gb.at[x, ymod(-2 * d), tail]
                bc[d, 3] = send(held, held, y_dev[d])
                held = gb.at[x, ymod(-2 * d), parts[d]]
                bc[d, 4] = send(held, held, y_far[d])
        for d in (1, -1) if s < 4 else (1,):
            b_cross(d * s, s > 2)

    def gz_step(s):
        for d in (1, -1):
            gz[d, s].wait_recv()
            if s == 2:
                held = ga.at[zmod(-2 * d), h]
                gz[d, 3] = send(held, held, z_dev[d])
                held = ga.at[zmod(-2 * d), h, zhalf[d]]
                gz[d, 4] = send(held, held, z_far[d])
        for d in (1, -1) if s < 4 else (1,):
            held = ga.at[zmod(-d * s), h]
            gs[d * s] = send(held, held, sibling)

    def a_step(s, rx):
        for d in (1, -1):
            if s == 0:
                if d == 1:
                    ax[rx].wait_recv()
            elif (d, s, rx) in ac:
                ac[d, s, rx].wait_recv()
            else:
                continue
            held = gb.at[xmod(-rx), ymod(-d * s), head]
            if s < 3:
                ac[d, s + 1, rx] = send(held, held, y_dev[d])
            if s == 2 and (rx in (0, 1)) == (d == 1):
                ac[d, 4, rx] = send(held, held, y_far[d])

    a_step(0, 1)
    a_step(0, -1)
    b_step(2)
    b_step(1)
    a_step(0, 2)
    b_relay(0)
    a_step(1, 0)
    gz_step(2)
    gz_step(1)
    a_step(1, 1)
    a_step(1, -1)
    b_step(3)
    b_step(4)
    a_step(1, 2)
    a_step(2, 0)
    b_relay(2)
    b_relay(-2)
    b_relay(1)
    b_relay(-1)
    a_step(2, 1)
    a_step(2, -1)
    gz_step(3)
    gz_step(4)
    a_step(2, 2)
    for s in (3, 4):
        for rx in (0, 1, -1, 2):
            a_step(s, rx)
    for copy in gs.values():
        copy.wait_recv()
    for (s, d), copy in bx.items():
        if abs(d) == 2 or abs(s) > 2:
            copy.wait_recv()

    def square(qq, total):
        xx, yy = qq // NYL, qq % NYL
        for half in range(2):
            right = jnp.concatenate(
                [gb[xx, 4 * half + yy], gb[xx, 4 * half + 2 + yy]], axis=0
            )
            total = total + jnp.dot(ga[qq, half], right, preferred_element_type=F32)
        return total

    total = jnp.zeros((R, W), F32)
    for qq in range(8):
        total = square(qq, total)
    poly = (quintic_b * gb[x, y].astype(F32) + quintic_c * total).astype(BF16)
    pb[q, h] = poly

    pc, ps = {}, {}
    for k in (2, 6, 1, 4, 3, 7, 5):
        pc[k] = send(pb.at[q, h], pb.at[q, h], q_dev(k))
    ps[0] = send(pb.at[q, h], pb.at[q, h], sibling)

    drain_at = len(pending) - 8
    for copy in pending[:drain_at]:
        copy.wait_send()
    del pending[:drain_at]
    for k in range(1, 8):
        for bit in range(2):
            rs_copy(q_of(k), q, bit).wait_send()
    for zz in range(NZ):
        for bit in range(2):
            sib_copy(zz, 2 * (1 - h) + bit).wait_send()

    def turn(qq, half):
        turned = pb[qq, half].astype(F32).T.astype(BF16)
        columns = pl.ds(pl.multiple_of(qq * R, R), R)
        for part in range(2):
            pt[2 * half + part, :, columns] = turned[part * R : (part + 1) * R]

    turn(q, h)

    def from_q(k):
        dx, dy = k // 2, k % 2
        return ((x - dx + NX) % NX) * NYL + (yl + dy) % NYL

    for k in (2, 6, 1, 4, 3, 7, 5):
        held = pb.at[from_q(k), h]
        pc[k].wait_recv()
        ps[k] = send(held, held, sibling)
        turn(from_q(k), h)
    for k in (0, 2, 6, 1, 4, 3, 7, 5):
        ps[k].wait_recv()
        turn(from_q(k), 1 - h)

    zr, yr = {}, {}

    def z_part(offsets):
        value = 0.0
        for half in range(2):
            left = jnp.concatenate([pb[zmod(a), half] for a in offsets], axis=0)
            right = xj[2 * half : 2 * half + 2, :, 0:CZ].reshape(W, CZ)
            value = value + jnp.dot(left, right, preferred_element_type=F32)
        for n, a in enumerate(offsets):
            zp[a % NZ] = value[n * R : (n + 1) * R]

    def y_part(offsets):
        left = jnp.concatenate([pt[yhmod(a)] for a in offsets], axis=0)
        right = xi[:, :, CZ:C].reshape(NZ * R, CY)
        value = jnp.dot(left, right, preferred_element_type=F32)
        for n, a in enumerate(offsets):
            yp[a % NYH] = value[n * R : (n + 1) * R]

    def first(d):
        return 0 if d == 1 else 1

    def z_send(d, s, c):
        n = 0 if d == 1 else 1
        value = zp[(d * (4 - s)) % NZ, halves[c]]
        for before in {2: (1, 0), 3: (2,)}.get(s, ()):
            if (d, before, c) in zr:
                zr[d, before, c].wait_recv()
                value = value + zs_in[n, before, halves[c]].astype(F32)
        zs_out[n, s, halves[c]] = value.astype(BF16)
        to = z_dev[d] if s else z_far[d]
        zr[d, s, c] = send(zs_out.at[n, s, halves[c]], zs_in.at[n, s, halves[c]], to)

    def y_send(d, s, c):
        n = 0 if d == 1 else 1
        value = yp[(d * (2 - s)) % NYH, halves[c]]
        if (d, s - 1, c) in yr:
            yr[d, s - 1, c].wait_recv()
            value = value + ys_in[n, s - 1, halves[c]].astype(F32)
        ys_out[n, s, halves[c]] = value.astype(BF16)
        yr[d, s, c] = send(ys_out.at[n, s, halves[c]], ys_in.at[n, s, halves[c]], yh_dev[d])

    def z_got(d, s, c):
        zr[d, s, c].wait_recv()
        return zs_in[0 if d == 1 else 1, s, halves[c]].astype(F32)

    def y_got(d, s, c):
        yr[d, s, c].wait_recv()
        return ys_in[0 if d == 1 else 1, s, halves[c]].astype(F32)

    z_part([4])
    for d in (1, -1):
        z_send(d, 0, first(d))
    y_part([2])
    for d in (1, -1):
        y_send(d, 0, first(d))
    z_part([3, -3])
    for c in (0, 1):
        for d in (1, -1):
            z_send(d, 1, first(d) if c == 0 else 1 - first(d))
    y_part([1, -1])
    for d in (1, -1):
        y_send(d, 1, 1 - first(d))
    z_part([2, -2])
    z_part([1, -1])
    for d in (1, -1):
        z_send(d, 2, first(d))
    for d in (1, -1):
        z_send(d, 2, 1 - first(d))
    for d in (1, -1):
        y_send(d, 1, first(d))
    y_part([0])
    z_part([0])
    for d in (1, -1):
        z_send(d, 3, first(d))
    for d in (1, -1):
        z_send(d, 3, 1 - first(d))
    scale = math.sqrt(max(M, N))
    for c in (0, 1):
        rows = halves[c]
        value = yp[0, rows] + y_got(1, 1, c) + y_got(-1, 1, c)
        out_ref[rows, CZ:C] = scale * (quintic_a * xi[z, rows, CZ:C].astype(F32) + value)
    for c in (0, 1):
        rows = halves[c]
        value = zp[0, rows] + z_got(1, 3, c) + z_got(-1, 3, c)
        out_ref[rows, 0:CZ] = scale * (quintic_a * xi[z, rows, 0:CZ].astype(F32) + value)

    for copy in pending:
        copy.wait_send()


def per_device(momentum):
    return pl.pallas_call(
        kernel,
        out_shape=jax.ShapeDtypeStruct((R, C), F32),
        in_specs=[pl.BlockSpec(memory_space=pl.ANY)],
        out_specs=pl.BlockSpec(memory_space=pltpu.VMEM),
        scratch_shapes=[
            pltpu.VMEM((NZ, R, C), BF16),
            pltpu.VMEM((NYH, R, C), BF16),
            pltpu.VMEM((NZ, 2, R, R), F32),
            pltpu.VMEM((NZ, NYH, R, R), F32),
            pltpu.VMEM((NZ, NYH, R, R), F32),
            pltpu.VMEM((2, R, R), F32),
            pltpu.VMEM((NZ, 2, R, R), BF16),
            pltpu.VMEM((NZ, 2, R, R), BF16),
            pltpu.VMEM((NZ, 2, R, W), BF16),
            pltpu.VMEM((NX, NY, R, W), BF16),
            pltpu.VMEM((NZ, 2, R, W), BF16),
            pltpu.VMEM((NYH, R, NZ * R), BF16),
            pltpu.VMEM((2, 4, R, CZ), BF16),
            pltpu.VMEM((2, 4, R, CZ), BF16),
            pltpu.VMEM((2, 2, R, CY), BF16),
            pltpu.VMEM((2, 2, R, CY), BF16),
            pltpu.VMEM((NZ, R, CZ), F32),
            pltpu.VMEM((NYH, R, CY), F32),
            pltpu.SemaphoreType.DMA((SEMS,)),
            pltpu.SemaphoreType.DMA((SEMS,)),
            pltpu.SemaphoreType.DMA((NZ, 2)),
            pltpu.SemaphoreType.DMA((NZ, 2)),
            pltpu.SemaphoreType.DMA((NZ, NYH)),
            pltpu.SemaphoreType.DMA((NZ, NYH)),
            pltpu.SemaphoreType.DMA((2,)),
        ],
        compiler_params=pltpu.CompilerParams(
            collective_id=0, has_side_effects=True, vmem_limit_bytes=60 * 1024 * 1024
        ),
        cost_estimate=pl.CostEstimate(flops=2200000000, bytes_accessed=1000000, transcendentals=0),
        name="newton_schulz",
    )(momentum)


def solution(mesh):
    return jax.shard_map(
        per_device, mesh=mesh, in_specs=(P("row", "col"),), out_specs=P("row", "col"), check_vma=False
    )
```

time: 99.6 us -> 92.5 us (0.929)
  Pallas kernels: 97.8 us -> 90.4 us
    pallas_call x1, Pallas kernels: 97.8 us -> 90.4 us  [per_device(): pl.pallas_call(kernel, out_shape=jax.ShapeDtypeStruct((R, C), F32), in_sp...]
where the time goes in v2:
time: 92.5 us; the launch traced here: 92.2 us
  Pallas kernels  90.4 us (98%)
  local copies, waits for them, and re-layouts  1.82 us (2%)
    pallas_call x1, Pallas kernels, per_device(): pl.pallas_call(kernel, out_shape=jax.ShapeDtypeStruct((R, C), F32), in_sp...  90.4 us

profile of v2, /device:TPU:1, one launch (start us, length us, event | category | flops | bytes accessed | tf_op | source)
XLA Modules:
  0.0 92.2 jit_solution(479494428942196703)
XLA Ops:
  0.0 90.4 %newton_schulz.1 = f32[128,896]{1,0:T(8,128)} custom-call(bf16[128,896]{1,0:T(8,128)(2,1)} %x_ref.1), custom_call_target="tpu_custom_call" | custom-call | flops 2200000000 | bytes 1000000 | tf_op jit(solution)/shard_map/newton_schulz/pallas_call | solution.py:480
  90.4 1.8 %copy.3 = f32[128,896]{1,0:T(8,128)} copy(f32[128,896]{1,0:T(8,128)} %newton_schulz.1) | data formatting | bytes 917504

commit v3 on v2

--- a/solution.py
+++ b/solution.py
@@ -198,15 +198,15 @@
     rs_step([1, -1, 0], near)
     gram([3, -3], near)
     rs_step([2, -2], near)
+    for c in (0, 2, 1, 3):
+        z_step(4, c)
+    gram([4], near)
+    rs_step([3, -3], near)
     y_step(2, 0)
     y_step(2, 1)
-    gram([3, -3, 0, 1, -1, 2, -2], [2])
-    rs_step([3, -3], near)
-    rs_step([3, -3, 0, 1, -1, 2, -2], [2])
-    for c in range(CHZ):
-        z_step(4, c)
-    gram([4], [0, 1, -1, 2])
-    rs_step([4], [0, 1, -1, 2])
+    gram([4, 3, -3, 0, 1, -1, 2, -2], [2])
+    rs_step([4], near)
+    rs_step([4, 3, -3, 0, 1, -1, 2, -2], [2])
     for k in (2, 6, 1, 4, 3, 7, 5):
         for bit in range(2):
             rs_copy(q_of(k), q_of(k), bit).wait_recv()
@@ -316,15 +316,15 @@
     b_step(4)
     a_step(1, 2)
     a_step(2, 0)
+    a_step(2, 1)
+    a_step(2, -1)
+    b_relay(1)
+    b_relay(-1)
     b_relay(2)
     b_relay(-2)
-    b_relay(1)
-    b_relay(-1)
-    a_step(2, 1)
-    a_step(2, -1)
+    a_step(2, 2)
     gz_step(3)
     gz_step(4)
-    a_step(2, 2)
     for s in (3, 4):
         for rx in (0, 1, -1, 2):
             a_step(s, rx)
@@ -510,7 +510,7 @@
             pltpu.SemaphoreType.DMA((2,)),
         ],
         compiler_params=pltpu.CompilerParams(
-            collective_id=0, has_side_effects=True, vmem_limit_bytes=60 * 1024 * 1024
+            collective_id=0, has_side_effects=True, vmem_limit_bytes=48 * 1024 * 1024
         ),
         cost_estimate=pl.CostEstimate(flops=2200000000, bytes_accessed=1000000, transcendentals=0),
         name="newton_schulz",

time: 92.5 us -> 89.9 us (0.972)
  Pallas kernels: 90.4 us -> 87.8 us
    pallas_call x1, Pallas kernels: 90.4 us -> 87.8 us  [per_device(): pl.pallas_call(kernel, out_shape=jax.ShapeDtypeStruct((R, C), F32), in_sp...]
where the time goes in v3:
time: 89.9 us; the launch traced here: 89.5 us
  Pallas kernels  87.8 us (98%)
  local copies, waits for them, and re-layouts  1.71 us (2%)
    pallas_call x1, Pallas kernels, per_device(): pl.pallas_call(kernel, out_shape=jax.ShapeDtypeStruct((R, C), F32), in_sp...  87.8 us

profile of v3, /device:TPU:1, one launch (start us, length us, event | category | flops | bytes accessed | tf_op | source)
XLA Modules:
  0.0 89.5 jit_solution(3362861173849393422)
XLA Ops:
  0.0 0.0 copy-start
  0.0 0.9 %copy-done = bf16[128,896]{1,0:T(8,128)(2,1)S(1)} copy-done((bf16[128,896]{1,0:T(8,128)(2,1)S(1)}, bf16[128,896]{1,0:T(8,128)(2,1)}, u32[]{:S(2)}) %copy-start) | copy-done | bytes 229400
  0.9 87.8 %newton_schulz.1 = f32[128,896]{1,0:T(8,128)S(1)} custom-call(bf16[128,896]{1,0:T(8,128)(2,1)S(1)} %copy-done), custom_call_target="tpu_custom_call" | custom-call | flops 2200000000 | bytes 1000000 | tf_op jit(solution)/shard_map/newton_schulz/pallas_call | solution.py:480
  88.7 0.8 copy.3
Async XLA Ops:
  0.0 0.9 %copy-start = (bf16[128,896]{1,0:T(8,128)(2,1)S(1)}, bf16[128,896]{1,0:T(8,128)(2,1)}, u32[]{:S(2)}) copy-start(bf16[128,896]{1,0:T(8,128)(2,1)} %x_ref.1) | copy-start | bytes 688132

commit v4 on v3

--- a/solution.py
+++ b/solution.py
@@ -256,7 +256,7 @@
         gz[d, 2] = send(mine, mine, z_far[d])
     for d in (1, -1):
         gz[d, 1] = send(mine, mine, z_dev[d])
-    b_cross(0, False)
+    b_cross(0, True)
     mine = gb.at[x, y, head]
     for d in (1, -1):
         ac[d, 1, 0] = send(mine, mine, y_dev[d])
@@ -306,7 +306,6 @@
     b_step(2)
     b_step(1)
     a_step(0, 2)
-    b_relay(0)
     a_step(1, 0)
     gz_step(2)
     gz_step(1)
@@ -331,7 +330,7 @@
     for copy in gs.values():
         copy.wait_recv()
     for (s, d), copy in bx.items():
-        if abs(d) == 2 or abs(s) > 2:
+        if s == 0 or abs(d) == 2 or abs(s) > 2:
             copy.wait_recv()
 
     def square(qq, total):

time: 89.9 us -> 89.9 us (level)
  no operation moved by 1% of the time
where the time goes in v4:
time: 89.9 us; the launch traced here: 89.8 us
  Pallas kernels  88 us (98%)
  local copies, waits for them, and re-layouts  1.71 us (2%)
    pallas_call x1, Pallas kernels, per_device(): pl.pallas_call(kernel, out_shape=jax.ShapeDtypeStruct((R, C), F32), in_sp...  88 us

profile of v4, /device:TPU:1, one launch (start us, length us, event | category | flops | bytes accessed | tf_op | source)
XLA Modules:
  0.0 89.8 jit_solution(12575848797564496538)
XLA Ops:
  0.0 0.0 copy-start
  0.0 0.9 %copy-done = bf16[128,896]{1,0:T(8,128)(2,1)S(1)} copy-done((bf16[128,896]{1,0:T(8,128)(2,1)S(1)}, bf16[128,896]{1,0:T(8,128)(2,1)}, u32[]{:S(2)}) %copy-start) | copy-done | bytes 229400
  0.9 88.0 %newton_schulz.1 = f32[128,896]{1,0:T(8,128)S(1)} custom-call(bf16[128,896]{1,0:T(8,128)(2,1)S(1)} %copy-done), custom_call_target="tpu_custom_call" | custom-call | flops 2200000000 | bytes 1000000 | tf_op jit(solution)/shard_map/newton_schulz/pallas_call | solution.py:479
  89.0 0.8 copy.3
Async XLA Ops:
  0.0 0.9 %copy-start = (bf16[128,896]{1,0:T(8,128)(2,1)S(1)}, bf16[128,896]{1,0:T(8,128)(2,1)}, u32[]{:S(2)}) copy-start(bf16[128,896]{1,0:T(8,128)(2,1)} %x_ref.1) | copy-start | bytes 688132
